TPU v7x, 512 devices: a whole 4x8x8 slice. The times are simulated.
512 devices in a mesh: frame: 64 (over y, z_lo, core), space: 8 (over x, z_hi).
Axes of the slice: x: 4, y: 8, z: 8 (z_hi: 2, z_lo: 4; z = z_hi * 4 + z_lo), core: 2. Of those that a mesh axis runs over, the one named last changes fastest.
Arguments:
- queries: bfloat16 [65536, 3072], P(('frame', 'space')), may hold values from -60 to 60
- keys: bfloat16 [65536, 3072], P(('frame', 'space')), may hold values from -6 to 6
- values: bfloat16 [65536, 3072], P(('frame', 'space')), may hold values from -6 to 6
- latent: bfloat16 [65536, 3072], P(('frame', 'space')), may hold values from -6 to 6
- step_gate: float32 [50, 3072], replicated, may hold values from 0.5 to 3
- levels: int32 [64], replicated, may hold values from 0 to 49
- context_start: int32 [64], replicated, may hold values from 0 to 7
- context_end: int32 [64], replicated, may hold values from 9 to 16
Outputs:
- queued: bfloat16 [65536, 3072], P(('frame', 'space'))
All inputs are finite; a program needn't handle non-finite values.
Results may differ from a plain program's by a relative error of at most 0.0034.
Values may be sent and summed in bfloat16 or wider, within the bound.
A program may use at most 64 MiB of HBM per device.

v0:
```python
import jax
import jax.numpy as jnp
from jax import lax
from jax.sharding import PartitionSpec as P

HEAD_DIM = 128
FRAMES_BLK = 16


def extended(cells, sides, width):
    for axis, dim in sides:
        count = lax.axis_size(axis)
        ends = count - 1
        head = lax.slice_in_dim(cells, 0, width, axis=dim)
        tail = lax.slice_in_dim(cells, cells.shape[dim] - width, cells.shape[dim], axis=dim)
        cells = jnp.concatenate(
            [
                lax.ppermute(tail, axis, [(i, (i + 1) % count) for i in range(ends)]),
                cells,
                lax.ppermute(head, axis, [((i + 1) % count, i) for i in range(ends)]),
            ],
            axis=dim,
        )
    return cells


def from_behind(x, axis, by):
    devices = lax.axis_size(axis)
    pairs = [(i, i + by) for i in range(devices) if 0 <= i + by < devices]
    return lax.ppermute(x, axis, pairs)


def pick_entry(table, where_at):
    index = jnp.arange(table.shape[0], dtype=jnp.int32)
    return jnp.sum(jnp.where(index == where_at, table, 0), axis=0)


def pick_row(table, where_at):
    index = jnp.arange(table.shape[0], dtype=jnp.int32)
    return jnp.sum(jnp.where((index == where_at)[:, None], table, 0.0), axis=0)


def on_device(queries, keys, values, latent, step_gate, levels, context_start, context_end):
    frame_at = lax.axis_index("frame")
    blocks = lax.axis_size("frame")
    q_heads, k_heads, v_heads = (
        lax.all_to_all(queries, "space", split_axis=1, concat_axis=0, tiled=True),
        lax.all_to_all(keys, "space", split_axis=1, concat_axis=0, tiled=True),
        lax.all_to_all(values, "space", split_axis=1, concat_axis=0, tiled=True),
    )
    block_tok = k_heads.shape[0]
    context = extended(jnp.stack([k_heads, v_heads]), (("frame", 1),), block_tok)
    frame_tok = block_tok // FRAMES_BLK
    first = pick_entry(context_start, frame_at) * frame_tok
    last = pick_entry(context_end, frame_at) * frame_tok
    column = jnp.arange(3 * block_tok, dtype=jnp.int32)
    before = (column < block_tok) & (column >= first) & (frame_at > 0)
    inside = (column >= block_tok) & (column < 2 * block_tok)
    after = (column >= 2 * block_tok) & (column - 2 * block_tok < last) & (frame_at < blocks - 1)
    visible = before | inside | after
    scale = HEAD_DIM ** (-0.5)
    q_block = min(512, block_tok)
    local_heads = q_heads.shape[1] // HEAD_DIM
    pieces = []
    for head in range(local_heads):
        lo = head * HEAD_DIM
        k_ctx = context[0, :, lo : lo + HEAD_DIM]
        v_ctx = context[1, :, lo : lo + HEAD_DIM]

        def attend(q_rows):
            scores = jnp.dot(q_rows, k_ctx.T, preferred_element_type=jnp.float32) * scale
            scores = jnp.where(visible[None, :], scores, -1e30)
            top = jnp.max(scores, axis=1, keepdims=True)
            expo = jnp.exp(scores - top)
            weights = (expo / jnp.sum(expo, axis=1, keepdims=True)).astype(jnp.bfloat16)
            return jnp.dot(weights, v_ctx, preferred_element_type=jnp.float32).astype(jnp.bfloat16)

        grouped = q_heads[:, lo : lo + HEAD_DIM].reshape(block_tok // q_block, q_block, HEAD_DIM)
        pieces.append(lax.map(attend, grouped).reshape(block_tok, HEAD_DIM))
    attended = jnp.concatenate(pieces, axis=1)
    back = lax.all_to_all(attended, "space", split_axis=0, concat_axis=1, tiled=True)
    gate = pick_row(step_gate, pick_entry(levels, frame_at))
    updated = (latent.astype(jnp.float32) + gate[None, :] * back.astype(jnp.float32)).astype(
        jnp.bfloat16
    )
    queued = from_behind(updated, "frame", 1)
    return queued


def solution(mesh):
    placed = (
        P(("frame", "space"), None),
        P(("frame", "space"), None),
        P(("frame", "space"), None),
        P(("frame", "space"), None),
        P(),
        P(),
        P(),
        P(),
    )
    return jax.shard_map(
        on_device,
        mesh=mesh,
        in_specs=placed,
        out_specs=P(("frame", "space"), None),
        check_vma=False,
    )
```

profile of v0, /device:TPU:41, one launch (start us, length us, event | category | flops | bytes accessed | tf_op | source)
XLA Modules:
  0.0 197.2 jit_solution(15160209289495446991)
XLA Ops:
  0.0 2.1 %copy.29 = bf16[16,8,8,384]{3,2,0,1:T(8,128)(2,1)} copy(bf16[16,8,8,384]{3,2,1,0:T(8,128)(2,1)} %bitcast.113) | data formatting | bytes 1572864 | tf_op jit(solution)/shard_map/all_to_all | solution.py:48
  2.1 12.6 %all-to-all-start.1 = ((bf16[128,8,384]{2,0,1:T(8,128)(2,1)}), bf16[128,8,384]{2,0,1:T(8,128)(2,1)S(1)}, u32[]{:S(2)}, u32[]{:S(2)}) async-start(bf16[128,8,384]{2,0,1:T(8,128)(2,1)} %bitcast.76), calls=%async_computation.1 | async-start | bytes 1572864 | tf_op jit(solution)/shard_map/all_to_all | solution.py:48
  14.7 2.1 %copy.28 = bf16[16,8,8,384]{3,2,0,1:T(8,128)(2,1)} copy(bf16[16,8,8,384]{3,2,1,0:T(8,128)(2,1)} %bitcast.114) | data formatting | bytes 1572864 | tf_op jit(solution)/shard_map/all_to_all | solution.py:49
  16.8 13.7 %all-to-all-done.1 = bf16[128,8,384]{2,0,1:T(8,128)(2,1)S(1)} async-done(((bf16[128,8,384]{2,0,1:T(8,128)(2,1)}), bf16[128,8,384]{2,0,1:T(8,128)(2,1)S(1)}, u32[]{:S(2)}, u32[]{:S(2)}) %all-to-all-start.1) | async-done | bytes 786464 | tf_op jit(solution)/shard_map/all_to_all | solution.py:48
  30.5 3.6 %all-to-all-start.2 = ((bf16[128,8,384]{2,0,1:T(8,128)(2,1)}), bf16[128,8,384]{2,0,1:T(8,128)(2,1)S(1)}, u32[]{:S(2)}, u32[]{:S(2)}) async-start(bf16[128,8,384]{2,0,1:T(8,128)(2,1)} %bitcast.75), calls=%async_computation.2 | async-start | bytes 1572864 | tf_op jit(solution)/shard_map/all_to_all | solution.py:49
  34.1 1.5 copy.18
  35.6 1.2 copy.19
  36.8 10.3 %all-to-all-done.2 = bf16[128,8,384]{2,0,1:T(8,128)(2,1)S(1)} async-done(((bf16[128,8,384]{2,0,1:T(8,128)(2,1)}), bf16[128,8,384]{2,0,1:T(8,128)(2,1)S(1)}, u32[]{:S(2)}, u32[]{:S(2)}) %all-to-all-start.2) | async-done | bytes 786464 | tf_op jit(solution)/shard_map/all_to_all | solution.py:49
  47.0 4.6 %all-to-all-start = ((bf16[128,8,384]{2,0,1:T(8,128)(2,1)}), bf16[128,8,384]{2,0,1:T(8,128)(2,1)S(1)}, u32[]{:S(2)}, u32[]{:S(2)}) async-start(bf16[128,8,384]{2,0,1:T(8,128)(2,1)} %copy.19), calls=%async_computation | async-start | bytes 1572864 | tf_op jit(solution)/shard_map/all_to_all | solution.py:47
  51.6 1.3 pad_maximum_fusion.1
  52.9 21.1 %collective-permute-start = (bf16[2,1024,384]{2,1,0:T(8,128)(2,1)}, bf16[2,1024,384]{2,1,0:T(8,128)(2,1)}, u32[]{:S(2)}, u32[]{:S(2)}) collective-permute-start(bf16[2,1024,384]{2,1,0:T(8,128)(2,1)} %pad_maximum_fusion.1), channel_id=1, source_target_pairs={{0,8},{8,16},{16,24},{24,32},{32,40},{40,48},{48,56},{56,64},{64,7... | collective-permute-start | bytes 4718600 | tf_op jit(solution)/shard_map/ppermute | solution.py:18
  74.1 1.9 collective-permute-start.1
  76.0 0.7 select_reduce_fusion.1
  78.1 35.3 %collective-permute-done = bf16[2,1024,384]{2,1,0:T(8,128)(2,1)} collective-permute-done((bf16[2,1024,384]{2,1,0:T(8,128)(2,1)}, bf16[2,1024,384]{2,1,0:T(8,128)(2,1)}, u32[]{:S(2)}, u32[]{:S(2)}) %collective-permute-start) | collective-permute-done | bytes 1572896 | tf_op jit(solution)/shard_map/ppermute | solution.py:18
  113.4 2.0 %collective-permute-done.1 = bf16[2,1024,384]{2,1,0:T(8,128)(2,1)} collective-permute-done((bf16[2,1024,384]{2,1,0:T(8,128)(2,1)}, bf16[2,1024,384]{2,1,0:T(8,128)(2,1)}, u32[]{:S(2)}, u32[]{:S(2)}) %collective-permute-start.1) | collective-permute-done | bytes 1572896 | tf_op jit(solution)/shard_map/ppermute | solution.py:20
  115.4 3.0 %pad_maximum_fusion = bf16[2,3072,384]{2,1,0:T(8,128)(2,1)S(1)} fusion(bf16[2,1024,384]{2,1,0:T(8,128)(2,1)} %collective-permute-done.1, bf16[1,1024,384]{2,1,0:T(8,128)(2,1)S(1)} %bitcast.104, bf16[1,1024,384]{2,1,0:T(8,128)(2,1)S(1)} %bitcast.102, bf16[2,1024,384]{2,1,0:T(8,128)(2,1)} %collective-permute-done), kind=kLoop, calls=%fused_computation.87 | loop fusion | flops 18874368 | bytes 9437184 | tf_op jit(solution)/shard_map/concatenate | solution.py:16
  118.4 2.0 %slice_bitcast_fusion.4 = (bf16[3072,128]{1,0:T(8,128)(2,1)}, bf16[3072,128]{1,0:T(8,128)(2,1)}, bf16[3072,128]{1,0:T(8,128)(2,1)S(1)}, bf16[3072,128]{1,0:T(8,1...) fusion(bf16[2,3072,384]{2,1,0:T(8,128)(2,1)S(1)} %pad_maximum_fusion), kind=kLoop, calls=%fused_computation.98 | loop fusion | bytes 9437184 | tf_op jit(solution)/shard_map/squeeze | solution.py:68
  120.4 9.6 %while.33 = (s32[]{:T(128)}, bf16[2,512,128]{2,1,0:T(8,128)(2,1)S(1)}, bf16[2,512,128]{2,1,0:T(8,128)(2,1)S(1)}, bf16[3072,128]{1,0:T(8,128)(2,1)S(1)}, bf16[307...) while((s32[]{:T(128)}, ...), condition=%wide.region_7.8_spmd.clone, body=%wide.region_4.0_spmd.clone.sunk | while | flops 824288256 | bytes 23877780 | solution.py:79
  120.4 1.2 fusion.93
  121.6 1.4 fusion.94
  123.0 2.1 %fusion.95 = bf16[2,512,128]{2,1,0:T(8,128)(2,1)S(1)} fusion(bf16[2,512,128]{2,1,0:T(8,128)(2,1)S(1)} %get-tuple-element.495, s32[]{:T(128)} %get-tuple-element.494, bf16[3072,128]{1,0:T(8,128)(2,1)S(1)} %copy-done.2, f32[512,3072]{1,0:T(8,128)S(1)} %get-tuple-element.400, f32[512]{0:T(512)S(1)} %fusion.94, f32[512]{0:T(512)S(1)} %get-tuple-element.401, ...), kind=kOutput, calls=%fused_computation.11.clone.1 | convolution fusion | flops 410583040 | bytes 7216132 | tf_op jit(solution)/shard_map/while/body/eval_jaxpr/dot_general | solution.py:76
  125.2 1.2 fusion.93
  126.4 1.4 fusion.94
  127.8 2.1 %fusion.95 = bf16[2,512,128]{2,1,0:T(8,128)(2,1)S(1)} fusion(bf16[2,512,128]{2,1,0:T(8,128)(2,1)S(1)} %get-tuple-element.495, s32[]{:T(128)} %get-tuple-element.494, bf16[3072,128]{1,0:T(8,128)(2,1)S(1)} %copy-done.2, f32[512,3072]{1,0:T(8,128)S(1)} %get-tuple-element.400, f32[512]{0:T(512)S(1)} %fusion.94, f32[512]{0:T(512)S(1)} %get-tuple-element.401, ...), kind=kOutput, calls=%fused_computation.11.clone.1 | convolution fusion | flops 410583040 | bytes 7216132 | tf_op jit(solution)/shard_map/while/body/eval_jaxpr/dot_general | solution.py:76
  130.0 9.6 %while.34 = (s32[]{:T(128)}, bf16[2,512,128]{2,1,0:T(8,128)(2,1)S(1)}, bf16[2,512,128]{2,1,0:T(8,128)(2,1)S(1)}, bf16[3072,128]{1,0:T(8,128)(2,1)S(1)}, bf16[307...) while((s32[]{:T(128)}, ...), condition=%wide.region_11.12_spmd.clone, body=%wide.region_8.11_spmd.clone.sunk | while | flops 824288256 | bytes 23877780 | solution.py:79
  130.1 1.2 fusion.99
  131.2 1.4 fusion.100
  132.7 2.1 %fusion.101 = bf16[2,512,128]{2,1,0:T(8,128)(2,1)S(1)} fusion(bf16[2,512,128]{2,1,0:T(8,128)(2,1)S(1)} %get-tuple-element.465, s32[]{:T(128)} %get-tuple-element.464, bf16[3072,128]{1,0:T(8,128)(2,1)S(1)} %copy-done.1, f32[512,3072]{1,0:T(8,128)S(1)} %get-tuple-element.411, f32[512]{0:T(512)S(1)} %fusion.100, f32[512]{0:T(512)S(1)} %get-tuple-element.412, ...), kind=kOutput, calls=%fused_computation.39.clone.1 | convolution fusion | flops 410583040 | bytes 7216132 | tf_op jit(solution)/shard_map/while/body/eval_jaxpr/dot_general | solution.py:76
  134.8 1.2 fusion.99
  136.0 1.4 fusion.100
  137.4 2.1 %fusion.101 = bf16[2,512,128]{2,1,0:T(8,128)(2,1)S(1)} fusion(bf16[2,512,128]{2,1,0:T(8,128)(2,1)S(1)} %get-tuple-element.465, s32[]{:T(128)} %get-tuple-element.464, bf16[3072,128]{1,0:T(8,128)(2,1)S(1)} %copy-done.1, f32[512,3072]{1,0:T(8,128)S(1)} %get-tuple-element.411, f32[512]{0:T(512)S(1)} %fusion.100, f32[512]{0:T(512)S(1)} %get-tuple-element.412, ...), kind=kOutput, calls=%fused_computation.39.clone.1 | convolution fusion | flops 410583040 | bytes 7216132 | tf_op jit(solution)/shard_map/while/body/eval_jaxpr/dot_general | solution.py:76
  139.7 9.9 %while.35 = (s32[]{:T(128)}, bf16[2,512,128]{2,1,0:T(8,128)(2,1)S(1)}, bf16[2,512,128]{2,1,0:T(8,128)(2,1)S(1)}, bf16[3072,128]{1,0:T(8,128)(2,1)S(1)}, bf16[307...) while((s32[]{:T(128)}, ...), condition=%wide.region_15.16_spmd.clone, body=%wide.region_12.15_spmd.clone.sunk | while | flops 824288256 | bytes 20732024 | solution.py:79
  139.9 1.2 fusion.105
  141.0 1.4 fusion.106
  142.5 2.2 %fusion.107 = bf16[2,512,128]{2,1,0:T(8,128)(2,1)S(1)} fusion(bf16[2,512,128]{2,1,0:T(8,128)(2,1)S(1)} %get-tuple-element.435, s32[]{:T(128)} %get-tuple-element.434, bf16[3072,128]{1,0:T(8,128)(2,1)S(1)} %get-tuple-element.448, f32[512,3072]{1,0:T(8,128)S(1)} %get-tuple-element.422, f32[512]{0:T(512)S(1)} %fusion.106, ...), kind=kOutput, calls=%fused_computation.67.clone.1 | convolution fusion | flops 410583040 | bytes 7216132 | tf_op jit(solution)/shard_map/while/body/eval_jaxpr/dot_general | solution.py:76
  144.7 1.2 fusion.105
  145.9 1.4 fusion.106
  147.3 2.2 %fusion.107 = bf16[2,512,128]{2,1,0:T(8,128)(2,1)S(1)} fusion(bf16[2,512,128]{2,1,0:T(8,128)(2,1)S(1)} %get-tuple-element.435, s32[]{:T(128)} %get-tuple-element.434, bf16[3072,128]{1,0:T(8,128)(2,1)S(1)} %get-tuple-element.448, f32[512,3072]{1,0:T(8,128)S(1)} %get-tuple-element.422, f32[512]{0:T(512)S(1)} %fusion.106, ...), kind=kOutput, calls=%fused_computation.67.clone.1 | convolution fusion | flops 410583040 | bytes 7216132 | tf_op jit(solution)/shard_map/while/body/eval_jaxpr/dot_general | solution.py:76
  149.6 1.0 pad_maximum_fusion.2
  150.6 9.3 %all-to-all-start.3 = ((bf16[8,128,384]{2,1,0:T(8,128)(2,1)}), bf16[8,128,384]{2,1,0:T(8,128)(2,1)S(1)}, u32[]{:S(2)}, u32[]{:S(2)}) async-start(bf16[8,128,384]{2,1,0:T(8,128)(2,1)} %pad_maximum_fusion.2), calls=%async_computation.3 | async-start | bytes 1572864 | tf_op jit(solution)/shard_map/all_to_all | solution.py:81
  159.9 1.5 copy.17
  161.4 0.7 select_reduce_fusion.3
  162.2 0.7 iota_compare_fusion.16
  162.9 1.2 select_reduce_fusion
  164.1 10.8 %all-to-all-done.3 = bf16[8,128,384]{2,1,0:T(8,128)(2,1)S(1)} async-done(((bf16[8,128,384]{2,1,0:T(8,128)(2,1)}), bf16[8,128,384]{2,1,0:T(8,128)(2,1)S(1)}, u32[]{:S(2)}, u32[]{:S(2)}) %all-to-all-start.3) | async-done | bytes 786464 | tf_op jit(solution)/shard_map/all_to_all | solution.py:81
  175.8 11.3 %collective-permute-start.2 = (bf16[128,3072]{0,1:T(8,128)(2,1)S(1)}, bf16[128,3072]{0,1:T(8,128)(2,1)S(1)}, u32[]{:S(2)}, u32[]{:S(2)}) collective-permute-start(bf16[128,3072]{0,1:T(8,128)(2,1)S(1)} %fusion.64), channel_id=1, source_target_pairs={{0,8},{8,16},{16,24},{24,32},{32,40},{40,48},{48,56},{56,64},{64,7... | collective-permute-start | bytes 2359304 | tf_op jit(solution)/shard_map/ppermute | solution.py:30
  187.1 8.9 %collective-permute-done.2 = bf16[128,3072]{0,1:T(8,128)(2,1)S(1)} collective-permute-done((bf16[128,3072]{0,1:T(8,128)(2,1)S(1)}, bf16[128,3072]{0,1:T(8,128)(2,1)S(1)}, u32[]{:S(2)}, u32[]{:S(2)}) %collective-permute-start.2) | collective-permute-done | bytes 786464 | tf_op jit(solution)/shard_map/ppermute | solution.py:30
  196.0 1.2 copy.23
  (29 shorter events, 1.2 us)
Async XLA Ops:
  2.1 73.9 %copy-start.3 = (s32[64]{0:T(128)S(1)}, s32[64]{0:T(128)}, u32[]{:S(2)}) copy-start(s32[64]{0:T(128)} %param.21) | copy-start | bytes 772
  2.1 73.9 %copy-start.4 = (s32[64]{0:T(128)S(1)}, s32[64]{0:T(128)}, u32[]{:S(2)}) copy-start(s32[64]{0:T(128)} %param.20) | copy-start | bytes 772
  2.1 28.4 %all-to-all-start.1 = ((bf16[128,8,384]{2,0,1:T(8,128)(2,1)}), bf16[128,8,384]{2,0,1:T(8,128)(2,1)S(1)}, u32[]{:S(2)}, u32[]{:S(2)}) async-start(bf16[128,8,384]{2,0,1:T(8,128)(2,1)} %bitcast.76), calls=%async_computation.1 | async-start | bytes 1572864 | tf_op jit(solution)/shard_map/all_to_all | solution.py:48
  30.5 16.5 %all-to-all-start.2 = ((bf16[128,8,384]{2,0,1:T(8,128)(2,1)}), bf16[128,8,384]{2,0,1:T(8,128)(2,1)S(1)}, u32[]{:S(2)}, u32[]{:S(2)}) async-start(bf16[128,8,384]{2,0,1:T(8,128)(2,1)} %bitcast.75), calls=%async_computation.2 | async-start | bytes 1572864 | tf_op jit(solution)/shard_map/all_to_all | solution.py:49
  47.0 30.9 %all-to-all-start = ((bf16[128,8,384]{2,0,1:T(8,128)(2,1)}), bf16[128,8,384]{2,0,1:T(8,128)(2,1)S(1)}, u32[]{:S(2)}, u32[]{:S(2)}) async-start(bf16[128,8,384]{2,0,1:T(8,128)(2,1)} %copy.19), calls=%async_computation | async-start | bytes 1572864 | tf_op jit(solution)/shard_map/all_to_all | solution.py:47
  52.9 60.5 %collective-permute-start = (bf16[2,1024,384]{2,1,0:T(8,128)(2,1)}, bf16[2,1024,384]{2,1,0:T(8,128)(2,1)}, u32[]{:S(2)}, u32[]{:S(2)}) collective-permute-start(bf16[2,1024,384]{2,1,0:T(8,128)(2,1)} %pad_maximum_fusion.1), channel_id=1, source_target_pairs={{0,8},{8,16},{16,24},{24,32},{32,40},{40,48},{48,56},{56,64},{64,7... | collective-permute-start | bytes 4718600 | tf_op jit(solution)/shard_map/ppermute | solution.py:18
  74.1 41.3 %collective-permute-start.1 = (bf16[2,1024,384]{2,1,0:T(8,128)(2,1)}, bf16[2,1024,384]{2,1,0:T(8,128)(2,1)}, u32[]{:S(2)}, u32[]{:S(2)}) collective-permute-start(bf16[2,1024,384]{2,1,0:T(8,128)(2,1)} %pad_maximum_fusion.1), channel_id=1, source_target_pairs={{8,0},{16,8},{24,16},{32,24},{40,32},{48,40},{56,48},{64,56},{72,6... | collective-permute-start | bytes 4718600 | tf_op jit(solution)/shard_map/ppermute | solution.py:20
  120.4 2.6 %copy-start.2 = (bf16[3072,128]{1,0:T(8,128)(2,1)S(1)}, bf16[3072,128]{1,0:T(8,128)(2,1)}, u32[]{:S(2)}) copy-start(bf16[3072,128]{1,0:T(8,128)(2,1)} %get-tuple-element.508) | copy-start | bytes 2359300 | tf_op jit(solution)/shard_map/while
  125.2 2.6 %copy-start.2 = (bf16[3072,128]{1,0:T(8,128)(2,1)S(1)}, bf16[3072,128]{1,0:T(8,128)(2,1)}, u32[]{:S(2)}) copy-start(bf16[3072,128]{1,0:T(8,128)(2,1)} %get-tuple-element.508) | copy-start | bytes 2359300 | tf_op jit(solution)/shard_map/while
  130.0 9.6 %copy-start = (bf16[3072,128]{1,0:T(8,128)(2,1)S(1)}, bf16[3072,128]{1,0:T(8,128)(2,1)}, u32[]{:S(2)}) copy-start(bf16[3072,128]{1,0:T(8,128)(2,1)} %get-tuple-element.428) | copy-start | bytes 2359300
  130.1 2.6 %copy-start.1 = (bf16[3072,128]{1,0:T(8,128)(2,1)S(1)}, bf16[3072,128]{1,0:T(8,128)(2,1)}, u32[]{:S(2)}) copy-start(bf16[3072,128]{1,0:T(8,128)(2,1)} %get-tuple-element.478) | copy-start | bytes 2359300 | tf_op jit(solution)/shard_map/while
  134.8 2.6 %copy-start.1 = (bf16[3072,128]{1,0:T(8,128)(2,1)S(1)}, bf16[3072,128]{1,0:T(8,128)(2,1)}, u32[]{:S(2)}) copy-start(bf16[3072,128]{1,0:T(8,128)(2,1)} %get-tuple-element.478) | copy-start | bytes 2359300 | tf_op jit(solution)/shard_map/while
  139.7 21.8 %copy-start.5 = (s32[64]{0:T(128)S(1)}, s32[64]{0:T(128)}, u32[]{:S(2)}) copy-start(s32[64]{0:T(128)} %param.19) | copy-start | bytes 772
  150.6 24.4 %all-to-all-start.3 = ((bf16[8,128,384]{2,1,0:T(8,128)(2,1)}), bf16[8,128,384]{2,1,0:T(8,128)(2,1)S(1)}, u32[]{:S(2)}, u32[]{:S(2)}) async-start(bf16[8,128,384]{2,1,0:T(8,128)(2,1)} %pad_maximum_fusion.2), calls=%async_computation.3 | async-start | bytes 1572864 | tf_op jit(solution)/shard_map/all_to_all | solution.py:81
  175.8 20.2 %collective-permute-start.2 = (bf16[128,3072]{0,1:T(8,128)(2,1)S(1)}, bf16[128,3072]{0,1:T(8,128)(2,1)S(1)}, u32[]{:S(2)}, u32[]{:S(2)}) collective-permute-start(bf16[128,3072]{0,1:T(8,128)(2,1)S(1)} %fusion.64), channel_id=1, source_target_pairs={{0,8},{8,16},{16,24},{24,32},{32,40},{40,48},{48,56},{56,64},{64,7... | collective-permute-start | bytes 2359304 | tf_op jit(solution)/shard_map/ppermute | solution.py:30
where the time goes:
time: 198 us; the launch traced here: 197 us
  waiting for transfers between devices  81.1 us (41%)
  starting transfers between devices  64.4 us (33%)
  matrix products  20 us (10%)
  other arithmetic  17.7 us (9%)
  local copies, waits for them, and re-layouts  12.2 us (6%)
    ppermute x1, waiting for transfers between devices, extended(): lax.ppermute(tail, axis, [(i, (i + 1) % count) for i in range(ends)])  35.3 us
    ppermute x1, starting transfers between devices, extended(): lax.ppermute(tail, axis, [(i, (i + 1) % count) for i in range(ends)])  21.1 us
    all_to_all x1, waiting for transfers between devices, on_device(): lax.all_to_all(keys, 'space', split_axis=1, concat_axis=0, tiled=True)  13.7 us
    dot_general x6, matrix products, attend(): jnp.dot(weights, v_ctx, preferred_element_type=jnp.float32)  13 us
    all_to_all x1, starting transfers between devices, on_device(): lax.all_to_all(keys, 'space', split_axis=1, concat_axis=0, tiled=True)  12.6 us
    ppermute x1, starting transfers between devices, from_behind(): return lax.ppermute(x, axis, pairs)  11.3 us
    all_to_all x1, waiting for transfers between devices, on_device(): lax.all_to_all(attended, 'space', split_axis=0, concat_axis=1, tiled=True)  10.8 us
    all_to_all x1, waiting for transfers between devices, on_device(): lax.all_to_all(values, 'space', split_axis=1, concat_axis=0, tiled=True)  10.3 us
  transfers between devices with their start and end apart: 7, of which 6 were waited for; matrix products, arithmetic and copies ran while one was open for 6% of the time, Pallas kernels for 0%

commit v1 on v0

v1 whole, which is shorter than its diff:
```python
import functools

import jax
import jax.numpy as jnp
from jax import lax
from jax.experimental import pallas as pl
from jax.experimental.pallas import tpu as pltpu
from jax.sharding import PartitionSpec as P

HEAD_DIM = 128
FRAME_TOK = 64
SLICE = 128
BLOCK = 1024
LOCAL_HEADS = 3
GROUP = LOCAL_HEADS * HEAD_DIM
Q_ROWS = 256
CHUNKS = BLOCK // Q_ROWS
LOG2E = 1.4426950408889634
SCALE2 = HEAD_DIM ** (-0.5) * LOG2E
HIDDEN = -1e30
MESH = pl.DeviceIdType.MESH
DISTANCES = (4, 3, 5, 2, 6, 1, 7, 0)


def wrap(a, n):
    return lax.rem(a + n, n)


def position():
    frame, space = lax.axis_index("frame"), lax.axis_index("space")
    return space // 2, frame // 8, lax.rem(frame // 2, 4) + 4 * lax.rem(space, 2), lax.rem(frame, 2)


def device(x, y, z, core):
    return (y * 8 + lax.rem(z, 4) * 2 + core, x * 2 + z // 4)


def following(pair, y, core):
    return (
        wrap(pair + core, 4),
        wrap(y + core * (pair // 3), 8),
        1 - core,
    )


def preceding(pair, y, core):
    back = 1 - core
    return (
        wrap(pair - back, 4),
        wrap(y - back * ((3 - pair) // 3), 8),
        1 - core,
    )


def worker(pair, y, core, group):
    return device(lax.rem(pair + group, 4), y, group, core)


def kernel(
    start_ref, end_ref, q_hbm, k_hbm, v_hbm, latent_hbm,
    att_hbm, lat_out_hbm,
    q_buf, k_buf, v_buf, o_buf, p_buf,
    in_send, in_recv, near_send, near_recv, o_send, o_recv, lat_send, lat_recv,
):
    x, y, z, core = position()
    z_lo, z_hi = lax.rem(z, 4), z // 4
    here = x * 2 + z_hi
    pair = wrap(x - lax.rem(z, 4), 4)
    block = y * 8 + pair * 2 + core
    after, before = following(pair, y, core), preceding(pair, y, core)
    next_worker, prev_worker = worker(*after, z), worker(*before, z)
    home_after, home_before = following(z_lo, y, core), preceding(z_lo, y, core)
    keeps = x == wrap(2 * z_lo, 4)

    def home(spot, slice_index):
        p, yy, cc = spot
        return device(slice_index // 2, yy, p + 4 * lax.rem(slice_index, 2), cc)

    barrier = pltpu.get_barrier_semaphore()

    def greet(target):
        pl.semaphore_signal(barrier, inc=1, device_id=target, device_id_type=MESH)

    for t in range(8):
        source = home((pair, y, core), t)
        pl.when(jnp.logical_not(keeps & (here == t)))(functools.partial(greet, source))
        greet(worker(*home_before, t))
    greet(prev_worker)
    greet(next_worker)
    greet(home(home_before, here))
    pl.semaphore_wait(barrier, jnp.where(keeps, 18, 19))

    arrays = ((k_hbm, k_buf, BLOCK), (v_hbm, v_buf, BLOCK), (q_hbm, q_buf, 0))

    def incoming(which, h, i):
        hbm, buf, row0 = arrays[which]
        group = lax.rem(z + DISTANCES[i], 8)
        return (
            hbm.at[:, pl.ds(pl.multiple_of(group * GROUP + h * HEAD_DIM, HEAD_DIM), HEAD_DIM)],
            buf.at[h, pl.ds(pl.multiple_of(row0 + here * SLICE, SLICE), SLICE)],
            worker(z_lo, y, core, group),
        )

    def in_copy(which, h, i):
        src, dst, target = incoming(which, h, i)
        return pltpu.make_async_remote_copy(
            src_ref=src, dst_ref=dst, send_sem=in_send.at[which, h, i], recv_sem=in_recv.at[which, h],
            device_id=target, device_id_type=MESH,
        )

    def own_copy(which, h, i):
        src, dst, _ = incoming(which, h, i)
        return pltpu.make_async_copy(src, dst, in_recv.at[which, h])

    for h in range(LOCAL_HEADS):
        for which in range(3):
            for i, distance in enumerate(DISTANCES):
                if distance == 0:
                    pl.when(keeps)(lambda: own_copy(which, h, i).start())
                    pl.when(jnp.logical_not(keeps))(lambda: in_copy(which, h, i).start())
                else:
                    in_copy(which, h, i).start()

    lat_copy = pltpu.make_async_remote_copy(
        src_ref=latent_hbm, dst_ref=lat_out_hbm, send_sem=lat_send, recv_sem=lat_recv,
        device_id=home(home_after, here), device_id_type=MESH,
    )
    lat_copy.start()

    def wait_in(which, h):
        _, buf, row0 = arrays[which]
        whole = buf.at[h, pl.ds(row0, BLOCK)]
        pltpu.make_async_copy(whole, whole, in_recv.at[which, h]).wait()

    def near_copy(which, h, side):
        _, buf, _ = arrays[which]
        return pltpu.make_async_remote_copy(
            src_ref=buf.at[h, pl.ds(BLOCK, BLOCK)],
            dst_ref=buf.at[h, pl.ds(0 if side else 2 * BLOCK, BLOCK)],
            send_sem=near_send.at[which, h, side], recv_sem=near_recv.at[which, h, side],
            device_id=next_worker if side else prev_worker, device_id_type=MESH,
        )

    def pass_on(which, h):
        wait_in(which, h)
        for side in range(2):
            near_copy(which, h, side).start()

    def o_copy(h, t):
        return pltpu.make_async_remote_copy(
            src_ref=o_buf.at[h, pl.ds(pl.multiple_of(t * SLICE, SLICE), SLICE)],
            dst_ref=att_hbm.at[:, pl.ds(pl.multiple_of(z * GROUP + h * HEAD_DIM, HEAD_DIM), HEAD_DIM)],
            send_sem=o_send.at[h, t], recv_sem=o_recv.at[h],
            device_id=home(after, t), device_id_type=MESH,
        )

    pass_on(0, 0)
    pass_on(1, 0)

    column = lax.broadcasted_iota(jnp.int32, (1, BLOCK), 1)
    first = start_ref[block] * FRAME_TOK
    last = end_ref[block] * FRAME_TOK
    hide_before = jnp.where((column >= first) & (block > 0), 0.0, HIDDEN)
    hide_after = jnp.where((column < last) & (block < 63), 0.0, HIDDEN)

    def step(n, carry):
        h, i = n // CHUNKS, lax.rem(n, CHUNKS)

        @pl.when(i == 0)
        def _():
            wait_in(2, h)
            for which in range(2):
                for side in range(2):
                    near_copy(which, h, side).wait_recv()

        for which in range(2):
            pl.when((i == 2 + which) & (h < LOCAL_HEADS - 1))(lambda: pass_on(which, h + 1))

        chunk = lax.rem(i + x + z, CHUNKS)
        rows = pl.ds(pl.multiple_of(chunk * Q_ROWS, Q_ROWS), Q_ROWS)
        q = q_buf[h, rows, :]
        parts = []
        for part, hide in ((0, hide_before), (1, None), (2, hide_after)):
            s = lax.dot_general(
                q, k_buf[h, pl.ds(part * BLOCK, BLOCK), :], (((1,), (1,)), ((), ())),
                preferred_element_type=jnp.float32,
            ) * SCALE2
            parts.append(s if hide is None else s + hide)
        top = functools.reduce(jnp.maximum, [jnp.max(s, axis=1, keepdims=True) for s in parts])
        parts = [jnp.exp2(s - top) for s in parts]
        total = sum(jnp.sum(e, axis=1, keepdims=True) for e in parts)
        inverse = 1.0 / total
        out = None
        for part, e in enumerate(parts):
            o = jnp.dot(
                (e * inverse).astype(jnp.bfloat16), v_buf[h, pl.ds(part * BLOCK, BLOCK), :],
                preferred_element_type=jnp.float32,
            )
            out = o if out is None else out + o
        o_buf[h, rows, :] = out.astype(jnp.bfloat16)
        for t in range(Q_ROWS // SLICE):
            o_copy(h, chunk * (Q_ROWS // SLICE) + t).start()
        return carry

    lax.fori_loop(0, LOCAL_HEADS * CHUNKS, step, 0)

    for h in range(LOCAL_HEADS):
        pltpu.make_async_copy(o_buf.at[h], o_buf.at[h], o_recv.at[h]).wait()
    lat_copy.wait()
    for h in range(LOCAL_HEADS):
        for t in range(8):
            o_copy(h, t).wait_send()
        for which in range(3):
            for i, distance in enumerate(DISTANCES):
                if distance == 0:
                    pl.when(jnp.logical_not(keeps))(lambda: in_copy(which, h, i).wait_send())
                else:
                    in_copy(which, h, i).wait_send()
            if which < 2:
                for side in range(2):
                    near_copy(which, h, side).wait_send()


def on_device(queries, keys, values, latent, step_gate, levels, context_start, context_end):
    any_spec = pl.BlockSpec(memory_space=pl.ANY)
    smem = pl.BlockSpec(memory_space=pltpu.SMEM)
    dma = pltpu.SemaphoreType.DMA
    rows = jax.ShapeDtypeStruct(latent.shape, jnp.bfloat16)
    attended, moved = pl.pallas_call(
        kernel,
        out_shape=(rows, rows),
        in_specs=[smem, smem] + [any_spec] * 4,
        out_specs=(any_spec, any_spec),
        scratch_shapes=[
            pltpu.VMEM((LOCAL_HEADS, BLOCK, HEAD_DIM), jnp.bfloat16),
            pltpu.VMEM((LOCAL_HEADS, 3 * BLOCK, HEAD_DIM), jnp.bfloat16),
            pltpu.VMEM((LOCAL_HEADS, 3 * BLOCK, HEAD_DIM), jnp.bfloat16),
            pltpu.VMEM((LOCAL_HEADS, BLOCK, HEAD_DIM), jnp.bfloat16),
            pltpu.VMEM((16, 128), jnp.bfloat16),
            dma((3, LOCAL_HEADS, 8)), dma((3, LOCAL_HEADS)),
            dma((2, LOCAL_HEADS, 2)), dma((2, LOCAL_HEADS, 2)),
            dma((LOCAL_HEADS, 8)), dma((LOCAL_HEADS,)),
            dma, dma,
        ],
        compiler_params=pltpu.CompilerParams(
            collective_id=0, has_side_effects=True, vmem_limit_bytes=48 << 20
        ),
        cost_estimate=pl.CostEstimate(flops=4 * BLOCK * 3 * BLOCK * GROUP, bytes_accessed=8 << 20, transcendentals=0),
        name="attend",
    )(context_start, context_end, queries, keys, values, latent)
    frame = lax.axis_index("frame")
    gate = step_gate[levels[jnp.maximum(frame - 1, 0)]]
    updated = moved.astype(jnp.float32) + gate[None, :] * attended.astype(jnp.float32)
    return jnp.where(frame > 0, updated, 0.0).astype(jnp.bfloat16)


def solution(mesh):
    tokens = P(("frame", "space"), None)
    return jax.shard_map(
        on_device,
        mesh=mesh,
        in_specs=(tokens,) * 4 + (P(),) * 4,
        out_specs=tokens,
        check_vma=False,
    )
```

time: 198 us -> 113 us (0.57)
  the two profiles are of different devices: /device:TPU:41 before, /device:TPU:4 now
where the time goes in v1:
time: 113 us
  Pallas kernels  102 us (90%)
  local copies, waits for them, and re-layouts  7.16 us (6%)
  between operations  1.98 us (2%)
  other arithmetic  1.17 us (1%)
    pallas_call x1, Pallas kernels, on_device(): pl.pallas_call(kernel, out_shape=(rows, rows), in_specs=[smem, smem] + [a...  102 us
    unnamed x14, local copies, waits for them, and re-layouts  5.84 us

profile of v1, /device:TPU:4, one launch (start us, length us, event | category | flops | bytes accessed | tf_op | source)
XLA Modules:
  0.0 112.7 jit_solution(18048273423140954867)
XLA Ops:
  0.0 0.0 copy-start
  0.0 1.3 %dynamic_slice.6 = s32[1]{0:T(128)} dynamic-slice(s32[64]{0:T(128)} %param.13, s32[]{:T(128)S(6)} %max.3), dynamic_slice_sizes={1} | dynamic-slice | bytes 12 | tf_op jit(solution)/shard_map/dynamic_slice | solution.py:252
  3.3 0.0 copy-done
  3.3 0.0 copy-start.1
  3.3 1.1 copy-done.1
  4.4 0.0 copy-start.2
  4.4 1.1 %copy-done.2 = bf16[128,3072]{1,0:T(8,128)(2,1)S(1)} copy-done((bf16[128,3072]{1,0:T(8,128)(2,1)S(1)}, bf16[128,3072]{1,0:T(8,128)(2,1)}, u32[]{:S(2)}) %copy-start.2) | copy-done | bytes 786456
  5.6 0.0 copy-start.3
  5.6 1.1 %copy-done.3 = bf16[128,3072]{1,0:T(8,128)(2,1)S(1)} copy-done((bf16[128,3072]{1,0:T(8,128)(2,1)S(1)}, bf16[128,3072]{1,0:T(8,128)(2,1)}, u32[]{:S(2)}) %copy-start.3) | copy-done | bytes 786456
  6.7 0.0 copy-start.4
  6.7 1.1 %copy-done.4 = bf16[128,3072]{1,0:T(8,128)(2,1)S(1)} copy-done((bf16[128,3072]{1,0:T(8,128)(2,1)S(1)}, bf16[128,3072]{1,0:T(8,128)(2,1)}, u32[]{:S(2)}) %copy-start.4) | copy-done | bytes 786456
  7.8 0.0 copy-start.5
  7.8 0.7 copy-done.5
  8.5 0.0 copy-start.6
  8.5 0.7 copy-done.6
  9.1 102.3 %attend.1 = (bf16[128,3072]{1,0:T(8,128)(2,1)S(1)}, bf16[128,3072]{1,0:T(8,128)(2,1)S(1)}) custom-call(s32[64]{0:T(128)S(1)} %copy-done.5, s32[64]{0:T(128)S(1)} %copy-done.6, bf16[128,3072]{1,0:T(8,128)(2,1)S(1)} %copy-done.1, bf16[128,3072]{1,0:T(8,128)(2,1)S(1)} %copy-done.2, bf16[128,3072]{1,0:T(8,128)(2,1)S(1)} %copy-done.3, bf16[128,3072]{1,0:T(8,128)(2,1)S(1)} %copy-done.4), custom_call_target="tpu_custom_call" | custom-call | flops 4831838208 | bytes 8388608 | tf_op jit(solution)/shard_map/attend/pallas_call | solution.py:229
  111.5 1.2 %select_convert_fusion = bf16[128,3072]{1,0:T(8,128)(2,1)} fusion(bf16[128,3072]{1,0:T(8,128)(2,1)S(1)} %get-tuple-element.8, bf16[128,3072]{1,0:T(8,128)(2,1)S(1)} %get-tuple-element.7, f32[3072]{0:T(1024)S(1)} %bitcast.2, pred[]{:T(512)S(6)} %gt.3), kind=kLoop, calls=%fused_computation | loop fusion | flops 2359296 | bytes 2371585 | tf_op jit(solution)/shard_map/convert_element_type | solution.py:254
  (1 shorter events, 0.0 us)
Async XLA Ops:
  0.0 3.3 %copy-start = (f32[50,3072]{1,0:T(8,128)S(1)}, f32[50,3072]{1,0:T(8,128)}, u32[]{:S(2)}) copy-start(f32[50,3072]{1,0:T(8,128)} %param.12) | copy-start | bytes 1843204
  3.3 1.1 %copy-start.1 = (bf16[128,3072]{1,0:T(8,128)(2,1)S(1)}, bf16[128,3072]{1,0:T(8,128)(2,1)}, u32[]{:S(2)}) copy-start(bf16[128,3072]{1,0:T(8,128)(2,1)} %q_hbm.1) | copy-start | bytes 2359300
  4.4 1.1 %copy-start.2 = (bf16[128,3072]{1,0:T(8,128)(2,1)S(1)}, bf16[128,3072]{1,0:T(8,128)(2,1)}, u32[]{:S(2)}) copy-start(bf16[128,3072]{1,0:T(8,128)(2,1)} %k_hbm.1) | copy-start | bytes 2359300
  5.6 1.1 %copy-start.3 = (bf16[128,3072]{1,0:T(8,128)(2,1)S(1)}, bf16[128,3072]{1,0:T(8,128)(2,1)}, u32[]{:S(2)}) copy-start(bf16[128,3072]{1,0:T(8,128)(2,1)} %v_hbm.1) | copy-start | bytes 2359300
  6.7 1.1 %copy-start.4 = (bf16[128,3072]{1,0:T(8,128)(2,1)S(1)}, bf16[128,3072]{1,0:T(8,128)(2,1)}, u32[]{:S(2)}) copy-start(bf16[128,3072]{1,0:T(8,128)(2,1)} %latent_hbm.1) | copy-start | bytes 2359300
  7.8 0.7 copy-start.5
  8.5 0.7 copy-start.6

commit v2 on v1

--- a/solution.py
+++ b/solution.py
@@ -18,6 +18,7 @@
 LOG2E = 1.4426950408889634
 SCALE2 = HEAD_DIM ** (-0.5) * LOG2E
 HIDDEN = -1e30
+KEYS, VALUES, QUERIES = 0, 1, 2
 MESH = pl.DeviceIdType.MESH
 DISTANCES = (4, 3, 5, 2, 6, 1, 7, 0)
 
@@ -57,10 +58,10 @@
 
 
 def kernel(
-    start_ref, end_ref, q_hbm, k_hbm, v_hbm, latent_hbm,
-    att_hbm, lat_out_hbm,
-    q_buf, k_buf, v_buf, o_buf, p_buf,
-    in_send, in_recv, near_send, near_recv, o_send, o_recv, lat_send, lat_recv,
+    start_hbm, end_hbm, levels_hbm, gate_hbm, q_hbm, k_hbm, v_hbm, latent_hbm,
+    att_hbm, lat_out_hbm, gate_ref,
+    q_buf, k_buf, v_buf, o_buf, gate_buf, start_ref, end_ref, levels_ref,
+    in_send, in_recv, near_send, near_recv, o_send, o_recv, lat_send, lat_recv, table_sem,
 ):
     x, y, z, core = position()
     z_lo, z_hi = lax.rem(z, 4), z // 4
@@ -76,6 +77,12 @@
         p, yy, cc = spot
         return device(slice_index // 2, yy, p + 4 * lax.rem(slice_index, 2), cc)
 
+    tables = [
+        pltpu.make_async_copy(src, dst, table_sem.at[i])
+        for i, (src, dst) in enumerate(
+            ((start_hbm, start_ref), (end_hbm, end_ref), (levels_hbm, levels_ref), (gate_hbm, gate_buf))
+        )
+    ]
     barrier = pltpu.get_barrier_semaphore()
 
     def greet(target):
@@ -112,21 +119,18 @@
         src, dst, _ = incoming(which, h, i)
         return pltpu.make_async_copy(src, dst, in_recv.at[which, h])
 
-    for h in range(LOCAL_HEADS):
-        for which in range(3):
-            for i, distance in enumerate(DISTANCES):
-                if distance == 0:
-                    pl.when(keeps)(lambda: own_copy(which, h, i).start())
-                    pl.when(jnp.logical_not(keeps))(lambda: in_copy(which, h, i).start())
-                else:
-                    in_copy(which, h, i).start()
+    def send_in(which, h):
+        for i, distance in enumerate(DISTANCES):
+            if distance == 0:
+                pl.when(keeps)(lambda: own_copy(which, h, i).start())
+                pl.when(jnp.logical_not(keeps))(lambda: in_copy(which, h, i).start())
+            else:
+                in_copy(which, h, i).start()
 
     lat_copy = pltpu.make_async_remote_copy(
         src_ref=latent_hbm, dst_ref=lat_out_hbm, send_sem=lat_send, recv_sem=lat_recv,
         device_id=home(home_after, here), device_id_type=MESH,
     )
-    lat_copy.start()
-
     def wait_in(which, h):
         _, buf, row0 = arrays[which]
         whole = buf.at[h, pl.ds(row0, BLOCK)]
@@ -154,8 +158,19 @@
             device_id=home(after, t), device_id_type=MESH,
         )
 
-    pass_on(0, 0)
-    pass_on(1, 0)
+    send_in(KEYS, 0)
+    send_in(VALUES, 0)
+    send_in(QUERIES, 0)
+    send_in(KEYS, 1)
+    for copy in tables:
+        copy.start()
+    pass_on(KEYS, 0)
+    send_in(VALUES, 1)
+    pass_on(VALUES, 0)
+    send_in(QUERIES, 1)
+    for copy in tables:
+        copy.wait()
+    gate_ref[...] = gate_buf[pl.ds(levels_ref[wrap(lax.axis_index("frame") - 1, 64)], 1), :]
 
     column = lax.broadcasted_iota(jnp.int32, (1, BLOCK), 1)
     first = start_ref[block] * FRAME_TOK
@@ -168,13 +183,22 @@
 
         @pl.when(i == 0)
         def _():
-            wait_in(2, h)
+            wait_in(QUERIES, h)
             for which in range(2):
                 for side in range(2):
                     near_copy(which, h, side).wait_recv()
 
-        for which in range(2):
-            pl.when((i == 2 + which) & (h < LOCAL_HEADS - 1))(lambda: pass_on(which, h + 1))
+        @pl.when((i == 2) & (h < LOCAL_HEADS - 1))
+        def _():
+            pass_on(KEYS, h + 1)
+            pl.when(h == 0)(lambda: send_in(KEYS, 2))
+            pl.when(h == 1)(lambda: send_in(QUERIES, 2))
+
+        @pl.when((i == 3) & (h < LOCAL_HEADS - 1))
+        def _():
+            pass_on(VALUES, h + 1)
+            pl.when(h == 0)(lambda: send_in(VALUES, 2))
+            pl.when(h == 1)(lambda: lat_copy.start())
 
         chunk = lax.rem(i + x + z, CHUNKS)
         rows = pl.ds(pl.multiple_of(chunk * Q_ROWS, Q_ROWS), Q_ROWS)
@@ -221,37 +245,47 @@
                     near_copy(which, h, side).wait_send()
 
 
-def on_device(queries, keys, values, latent, step_gate, levels, context_start, context_end):
+def run_kernel(
+    context_start, context_end, queries, keys, values, latent, step_gate, levels, name="attend", cid=0
+):
     any_spec = pl.BlockSpec(memory_space=pl.ANY)
-    smem = pl.BlockSpec(memory_space=pltpu.SMEM)
     dma = pltpu.SemaphoreType.DMA
     rows = jax.ShapeDtypeStruct(latent.shape, jnp.bfloat16)
-    attended, moved = pl.pallas_call(
+    return pl.pallas_call(
         kernel,
-        out_shape=(rows, rows),
-        in_specs=[smem, smem] + [any_spec] * 4,
-        out_specs=(any_spec, any_spec),
+        out_shape=(rows, rows, jax.ShapeDtypeStruct((1, step_gate.shape[1]), jnp.float32)),
+        in_specs=[any_spec] * 8,
+        out_specs=(any_spec, any_spec, pl.BlockSpec(memory_space=pltpu.VMEM)),
         scratch_shapes=[
             pltpu.VMEM((LOCAL_HEADS, BLOCK, HEAD_DIM), jnp.bfloat16),
             pltpu.VMEM((LOCAL_HEADS, 3 * BLOCK, HEAD_DIM), jnp.bfloat16),
             pltpu.VMEM((LOCAL_HEADS, 3 * BLOCK, HEAD_DIM), jnp.bfloat16),
             pltpu.VMEM((LOCAL_HEADS, BLOCK, HEAD_DIM), jnp.bfloat16),
-            pltpu.VMEM((16, 128), jnp.bfloat16),
+            pltpu.VMEM(step_gate.shape, jnp.float32),
+            pltpu.SMEM(context_start.shape, jnp.int32),
+            pltpu.SMEM(context_end.shape, jnp.int32),
+            pltpu.SMEM(levels.shape, jnp.int32),
             dma((3, LOCAL_HEADS, 8)), dma((3, LOCAL_HEADS)),
             dma((2, LOCAL_HEADS, 2)), dma((2, LOCAL_HEADS, 2)),
             dma((LOCAL_HEADS, 8)), dma((LOCAL_HEADS,)),
-            dma, dma,
+            dma, dma, dma((4,)),
         ],
         compiler_params=pltpu.CompilerParams(
-            collective_id=0, has_side_effects=True, vmem_limit_bytes=48 << 20
+            collective_id=cid, has_side_effects=True, vmem_limit_bytes=61000 << 10
         ),
-        cost_estimate=pl.CostEstimate(flops=4 * BLOCK * 3 * BLOCK * GROUP, bytes_accessed=8 << 20, transcendentals=0),
-        name="attend",
-    )(context_start, context_end, queries, keys, values, latent)
-    frame = lax.axis_index("frame")
-    gate = step_gate[levels[jnp.maximum(frame - 1, 0)]]
-    updated = moved.astype(jnp.float32) + gate[None, :] * attended.astype(jnp.float32)
-    return jnp.where(frame > 0, updated, 0.0).astype(jnp.bfloat16)
+        cost_estimate=pl.CostEstimate(
+            flops=4 * BLOCK * 3 * BLOCK * GROUP, bytes_accessed=8 << 20, transcendentals=0
+        ),
+        name=name,
+    )(context_start, context_end, levels, step_gate, queries, keys, values, latent)
+
+
+def on_device(queries, keys, values, latent, step_gate, levels, context_start, context_end):
+    attended, moved, gate = run_kernel(
+        context_start, context_end, queries, keys, values, latent, step_gate, levels
+    )
+    updated = moved.astype(jnp.float32) + gate * attended.astype(jnp.float32)
+    return jnp.where(lax.axis_index("frame") > 0, updated, 0.0).astype(jnp.bfloat16)
 
 
 def solution(mesh):

time: 113 us -> 106 us (0.938)
  local copies, waits for them, and re-layouts: 7.16 us -> 0 us
  between operations: 1.98 us -> 0.01 us
  other arithmetic: 1.17 us -> 2.54 us
    unnamed x14 -> x0, local copies, waits for them, and re-layouts: 5.84 us -> none
    convert_element_type x1, other arithmetic: 1.17 us -> 2.54 us  [on_device(): jnp.where(lax.axis_index('frame') > 0, updated, 0.0).astype(jnp.bfloat16)]
    dynamic_slice x2 -> x0, local copies, waits for them, and re-layouts: 1.32 us -> none  [on_device(): gate = step_gate[levels[jnp.maximum(frame - 1, 0)]]]
where the time goes in v2:
time: 106 us; the launch traced here: 105 us
  Pallas kernels  103 us (97%)
  other arithmetic  2.54 us (2%)
    pallas_call x1, Pallas kernels, run_kernel(): pl.pallas_call(kernel, out_shape=(rows, rows, jax.ShapeDtypeStruct((1, st...  103 us
    convert_element_type x1, other arithmetic, on_device(): jnp.where(lax.axis_index('frame') > 0, updated, 0.0).astype(jnp.bfloat16)  2.54 us

profile of v2, /device:TPU:4, one launch (start us, length us, event | category | flops | bytes accessed | tf_op | source)
XLA Modules:
  0.0 105.4 jit_solution(11119402822222306685)
XLA Ops:
  0.0 102.9 %attend.1 = (bf16[128,3072]{1,0:T(8,128)(2,1)}, bf16[128,3072]{1,0:T(8,128)(2,1)}, f32[1,3072]{1,0:T(1,128)}) custom-call(s32[64]{0:T(128)} %start_hbm.1, s32[64]{0:T(128)} %end_hbm.1, s32[64]{0:T(128)} %levels_hbm.1, f32[50,3072]{1,0:T(8,128)} %gate_hbm.1, bf16[128,3072]{1,0:T(8,128)(2,1)} %q_hbm.1, bf16[128,3072]{1,0:T(8,128)(2,1)} %k_hbm.1, ...), custom_call_target="tpu_custom_call" | custom-call | flops 4831838208 | bytes 8388608 | tf_op jit(solution)/shard_map/attend/pallas_call | solution.py:254
  102.9 2.5 %select_convert_fusion = bf16[128,3072]{1,0:T(8,128)(2,1)} fusion(bf16[128,3072]{1,0:T(8,128)(2,1)} %get-tuple-element.10, bf16[128,3072]{1,0:T(8,128)(2,1)} %get-tuple-element.8, f32[3072]{0:T(1024)} %bitcast.1, pred[]{:T(512)S(6)} %gt.3), kind=kLoop, calls=%fused_computation | loop fusion | flops 2359296 | bytes 2371585 | tf_op jit(solution)/shard_map/convert_element_type | solution.py:288

commit v3 on v2

--- a/solution.py
+++ b/solution.py
@@ -20,7 +20,9 @@
 HIDDEN = -1e30
 KEYS, VALUES, QUERIES = 0, 1, 2
 MESH = pl.DeviceIdType.MESH
-DISTANCES = (4, 3, 5, 2, 6, 1, 7, 0)
+PEERS = 8
+LAT_PARTS = 3
+NEAR_PARTS = 8
 
 
 def wrap(a, n):
@@ -53,8 +55,12 @@
     )
 
 
+def offset(group):
+    return 2 * lax.rem(group, 2)
+
+
 def worker(pair, y, core, group):
-    return device(lax.rem(pair + group, 4), y, group, core)
+    return device(lax.rem(pair + offset(group), 4), y, group, core)
 
 
 def kernel(
@@ -66,12 +72,12 @@
     x, y, z, core = position()
     z_lo, z_hi = lax.rem(z, 4), z // 4
     here = x * 2 + z_hi
-    pair = wrap(x - lax.rem(z, 4), 4)
+    pair = wrap(x - offset(z), 4)
     block = y * 8 + pair * 2 + core
     after, before = following(pair, y, core), preceding(pair, y, core)
     next_worker, prev_worker = worker(*after, z), worker(*before, z)
     home_after, home_before = following(z_lo, y, core), preceding(z_lo, y, core)
-    keeps = x == wrap(2 * z_lo, 4)
+    keeps = x == lax.rem(z_lo + offset(z), 4)
 
     def home(spot, slice_index):
         p, yy, cc = spot
@@ -99,9 +105,22 @@
 
     arrays = ((k_hbm, k_buf, BLOCK), (v_hbm, v_buf, BLOCK), (q_hbm, q_buf, 0))
 
+    def distance(i):
+        turn = lax.rem(i // 2 + x, 4)
+        along = 3 - turn if i % 2 else 4 + turn
+        return lax.rem(jnp.where(core == 0, along, 8 - along), 8)
+
+    def served(i, act_here, act_there):
+        if i % 2:
+            mine = keeps & (distance(i) == 0)
+            pl.when(mine)(act_here)
+            pl.when(jnp.logical_not(mine))(act_there)
+        else:
+            act_there()
+
     def incoming(which, h, i):
         hbm, buf, row0 = arrays[which]
-        group = lax.rem(z + DISTANCES[i], 8)
+        group = lax.rem(z + distance(i), 8)
         return (
             hbm.at[:, pl.ds(pl.multiple_of(group * GROUP + h * HEAD_DIM, HEAD_DIM), HEAD_DIM)],
             buf.at[h, pl.ds(pl.multiple_of(row0 + here * SLICE, SLICE), SLICE)],
@@ -120,35 +139,38 @@
         return pltpu.make_async_copy(src, dst, in_recv.at[which, h])
 
     def send_in(which, h):
-        for i, distance in enumerate(DISTANCES):
-            if distance == 0:
-                pl.when(keeps)(lambda: own_copy(which, h, i).start())
-                pl.when(jnp.logical_not(keeps))(lambda: in_copy(which, h, i).start())
-            else:
-                in_copy(which, h, i).start()
-
-    lat_copy = pltpu.make_async_remote_copy(
-        src_ref=latent_hbm, dst_ref=lat_out_hbm, send_sem=lat_send, recv_sem=lat_recv,
-        device_id=home(home_after, here), device_id_type=MESH,
-    )
+        for i in range(PEERS):
+            served(i, lambda: own_copy(which, h, i).start(), lambda: in_copy(which, h, i).start())
+
+    def lat_copy(part):
+        width = latent_hbm.shape[1] // LAT_PARTS
+        columns = pl.ds(pl.multiple_of(part * width, HEAD_DIM), width)
+        return pltpu.make_async_remote_copy(
+            src_ref=latent_hbm.at[:, columns], dst_ref=lat_out_hbm.at[:, columns],
+            send_sem=lat_send.at[part], recv_sem=lat_recv.at[part],
+            device_id=home(home_after, here), device_id_type=MESH,
+        )
+
     def wait_in(which, h):
         _, buf, row0 = arrays[which]
         whole = buf.at[h, pl.ds(row0, BLOCK)]
         pltpu.make_async_copy(whole, whole, in_recv.at[which, h]).wait()
 
-    def near_copy(which, h, side):
+    def near_copy(which, h, side, row=0, rows=BLOCK):
         _, buf, _ = arrays[which]
+        to = 0 if side else 2 * BLOCK
         return pltpu.make_async_remote_copy(
-            src_ref=buf.at[h, pl.ds(BLOCK, BLOCK)],
-            dst_ref=buf.at[h, pl.ds(0 if side else 2 * BLOCK, BLOCK)],
+            src_ref=buf.at[h, pl.ds(BLOCK + row, rows)],
+            dst_ref=buf.at[h, pl.ds(to + row, rows)],
             send_sem=near_send.at[which, h, side], recv_sem=near_recv.at[which, h, side],
             device_id=next_worker if side else prev_worker, device_id_type=MESH,
         )
 
     def pass_on(which, h):
         wait_in(which, h)
-        for side in range(2):
-            near_copy(which, h, side).start()
+        for piece in range(NEAR_PARTS):
+            for side in range(2):
+                near_copy(which, h, side, piece * (BLOCK // NEAR_PARTS), BLOCK // NEAR_PARTS).start()
 
     def o_copy(h, t):
         return pltpu.make_async_remote_copy(
@@ -158,19 +180,18 @@
             device_id=home(after, t), device_id_type=MESH,
         )
 
-    send_in(KEYS, 0)
-    send_in(VALUES, 0)
-    send_in(QUERIES, 0)
-    send_in(KEYS, 1)
+    for h in range(LOCAL_HEADS):
+        for which in (KEYS, VALUES, QUERIES):
+            send_in(which, h)
     for copy in tables:
         copy.start()
     pass_on(KEYS, 0)
-    send_in(VALUES, 1)
     pass_on(VALUES, 0)
-    send_in(QUERIES, 1)
+    lat_copy(0).start()
     for copy in tables:
         copy.wait()
-    gate_ref[...] = gate_buf[pl.ds(levels_ref[wrap(lax.axis_index("frame") - 1, 64)], 1), :]
+    level = levels_ref[wrap(lax.axis_index("frame") - 1, 64)]
+    gate_ref[...] = jnp.broadcast_to(gate_buf[pl.ds(level, 1), :], gate_ref.shape)
 
     column = lax.broadcasted_iota(jnp.int32, (1, BLOCK), 1)
     first = start_ref[block] * FRAME_TOK
@@ -191,14 +212,11 @@
         @pl.when((i == 2) & (h < LOCAL_HEADS - 1))
         def _():
             pass_on(KEYS, h + 1)
-            pl.when(h == 0)(lambda: send_in(KEYS, 2))
-            pl.when(h == 1)(lambda: send_in(QUERIES, 2))
 
         @pl.when((i == 3) & (h < LOCAL_HEADS - 1))
         def _():
             pass_on(VALUES, h + 1)
-            pl.when(h == 0)(lambda: send_in(VALUES, 2))
-            pl.when(h == 1)(lambda: lat_copy.start())
+            lat_copy(h + 1).start()
 
         chunk = lax.rem(i + x + z, CHUNKS)
         rows = pl.ds(pl.multiple_of(chunk * Q_ROWS, Q_ROWS), Q_ROWS)
@@ -230,16 +248,14 @@
 
     for h in range(LOCAL_HEADS):
         pltpu.make_async_copy(o_buf.at[h], o_buf.at[h], o_recv.at[h]).wait()
-    lat_copy.wait()
+    for part in range(LAT_PARTS):
+        lat_copy(part).wait()
     for h in range(LOCAL_HEADS):
         for t in range(8):
             o_copy(h, t).wait_send()
         for which in range(3):
-            for i, distance in enumerate(DISTANCES):
-                if distance == 0:
-                    pl.when(jnp.logical_not(keeps))(lambda: in_copy(which, h, i).wait_send())
-                else:
-                    in_copy(which, h, i).wait_send()
+            for i in range(PEERS):
+                served(i, lambda: None, lambda: in_copy(which, h, i).wait_send())
             if which < 2:
                 for side in range(2):
                     near_copy(which, h, side).wait_send()
@@ -253,7 +269,7 @@
     rows = jax.ShapeDtypeStruct(latent.shape, jnp.bfloat16)
     return pl.pallas_call(
         kernel,
-        out_shape=(rows, rows, jax.ShapeDtypeStruct((1, step_gate.shape[1]), jnp.float32)),
+        out_shape=(rows, rows, jax.ShapeDtypeStruct((8, step_gate.shape[1]), jnp.float32)),
         in_specs=[any_spec] * 8,
         out_specs=(any_spec, any_spec, pl.BlockSpec(memory_space=pltpu.VMEM)),
         scratch_shapes=[
@@ -268,7 +284,7 @@
             dma((3, LOCAL_HEADS, 8)), dma((3, LOCAL_HEADS)),
             dma((2, LOCAL_HEADS, 2)), dma((2, LOCAL_HEADS, 2)),
             dma((LOCAL_HEADS, 8)), dma((LOCAL_HEADS,)),
-            dma, dma, dma((4,)),
+            dma((LAT_PARTS,)), dma((LAT_PARTS,)), dma((4,)),
         ],
         compiler_params=pltpu.CompilerParams(
             collective_id=cid, has_side_effects=True, vmem_limit_bytes=61000 << 10
@@ -284,8 +300,10 @@
     attended, moved, gate = run_kernel(
         context_start, context_end, queries, keys, values, latent, step_gate, levels
     )
-    updated = moved.astype(jnp.float32) + gate * attended.astype(jnp.float32)
-    return jnp.where(lax.axis_index("frame") > 0, updated, 0.0).astype(jnp.bfloat16)
+    tiles = (latent.shape[0] // 8, 8, latent.shape[1])
+    updated = moved.reshape(tiles).astype(jnp.float32) + gate * attended.reshape(tiles).astype(jnp.float32)
+    queued = jnp.where(lax.axis_index("frame") > 0, updated, 0.0).astype(jnp.bfloat16)
+    return queued.reshape(latent.shape)
 
 
 def solution(mesh):

time: 106 us -> 104 us (0.981)
  the two profiles are of different devices: /device:TPU:4 before, /device:TPU:1 now
where the time goes in v3:
time: 104 us; the launch traced here: 103 us
  Pallas kernels  101 us (97%)
  other arithmetic  2.54 us (2%)
    pallas_call x1, Pallas kernels, run_kernel(): pl.pallas_call(kernel, out_shape=(rows, rows, jax.ShapeDtypeStruct((8, st...  101 us
    convert_element_type x1, other arithmetic, on_device(): jnp.where(lax.axis_index('frame') > 0, updated, 0.0).astype(jnp.bfloat16)  2.54 us

profile of v3, /device:TPU:1, one launch (start us, length us, event | category | flops | bytes accessed | tf_op | source)
XLA Modules:
  0.0 103.3 jit_solution(16451653535799182425)
XLA Ops:
  0.0 100.7 %attend.1 = (bf16[128,3072]{1,0:T(8,128)(2,1)}, bf16[128,3072]{1,0:T(8,128)(2,1)}, f32[8,3072]{1,0:T(8,128)}) custom-call(s32[64]{0:T(128)} %start_hbm.1, s32[64]{0:T(128)} %end_hbm.1, s32[64]{0:T(128)} %levels_hbm.1, f32[50,3072]{1,0:T(8,128)} %gate_hbm.1, bf16[128,3072]{1,0:T(8,128)(2,1)} %q_hbm.1, bf16[128,3072]{1,0:T(8,128)(2,1)} %k_hbm.1, ...), custom_call_target="tpu_custom_call" | custom-call | flops 4831838208 | bytes 8388608 | tf_op jit(solution)/shard_map/attend/pallas_call | solution.py:270
  100.7 2.5 %fusion.2 = bf16[128,3072]{1,0:T(8,128)(2,1)} fusion(bf16[128,3072]{1,0:T(8,128)(2,1)} %get-tuple-element.10, bf16[128,3072]{1,0:T(8,128)(2,1)} %get-tuple-element.8, f32[8,3072]{1,0:T(8,128)} %get-tuple-element.9, pred[]{:T(512)S(6)} %gt.3), kind=kLoop, calls=%fused_computation.3 | loop fusion | flops 2359296 | bytes 2457601 | tf_op jit(solution)/shard_map/convert_element_type | solution.py:305

commit v4 on v3

--- a/solution.py
+++ b/solution.py
@@ -183,11 +183,12 @@
     for h in range(LOCAL_HEADS):
         for which in (KEYS, VALUES, QUERIES):
             send_in(which, h)
+            if which == VALUES:
+                lat_copy(h).start()
     for copy in tables:
         copy.start()
     pass_on(KEYS, 0)
     pass_on(VALUES, 0)
-    lat_copy(0).start()
     for copy in tables:
         copy.wait()
     level = levels_ref[wrap(lax.axis_index("frame") - 1, 64)]
@@ -216,7 +217,6 @@
         @pl.when((i == 3) & (h < LOCAL_HEADS - 1))
         def _():
             pass_on(VALUES, h + 1)
-            lat_copy(h + 1).start()
 
         chunk = lax.rem(i + x + z, CHUNKS)
         rows = pl.ds(pl.multiple_of(chunk * Q_ROWS, Q_ROWS), Q_ROWS)

time: 104 us -> 104 us (level)
  no operation moved by 1% of the time
where the time goes in v4:
time: 104 us
  Pallas kernels  101 us (97%)
  other arithmetic  2.54 us (2%)
    pallas_call x1, Pallas kernels, run_kernel(): pl.pallas_call(kernel, out_shape=(rows, rows, jax.ShapeDtypeStruct((8, st...  101 us
    convert_element_type x1, other arithmetic, on_device(): jnp.where(lax.axis_index('frame') > 0, updated, 0.0).astype(jnp.bfloat16)  2.54 us

profile of v4, /device:TPU:1, one launch (start us, length us, event | category | flops | bytes accessed | tf_op | source)
XLA Modules:
  0.0 103.7 jit_solution(16901217971411321845)
XLA Ops:
  0.0 101.2 %attend.1 = (bf16[128,3072]{1,0:T(8,128)(2,1)}, bf16[128,3072]{1,0:T(8,128)(2,1)}, f32[8,3072]{1,0:T(8,128)}) custom-call(s32[64]{0:T(128)} %start_hbm.1, s32[64]{0:T(128)} %end_hbm.1, s32[64]{0:T(128)} %levels_hbm.1, f32[50,3072]{1,0:T(8,128)} %gate_hbm.1, bf16[128,3072]{1,0:T(8,128)(2,1)} %q_hbm.1, bf16[128,3072]{1,0:T(8,128)(2,1)} %k_hbm.1, ...), custom_call_target="tpu_custom_call" | custom-call | flops 4831838208 | bytes 8388608 | tf_op jit(solution)/shard_map/attend/pallas_call | solution.py:270
  101.2 2.5 %fusion.2 = bf16[128,3072]{1,0:T(8,128)(2,1)} fusion(bf16[128,3072]{1,0:T(8,128)(2,1)} %get-tuple-element.10, bf16[128,3072]{1,0:T(8,128)(2,1)} %get-tuple-element.8, f32[8,3072]{1,0:T(8,128)} %get-tuple-element.9, pred[]{:T(512)S(6)} %gt.3), kind=kLoop, calls=%fused_computation.3 | loop fusion | flops 2359296 | bytes 2457601 | tf_op jit(solution)/shard_map/convert_element_type | solution.py:305

commit v5 on v4

--- a/solution.py
+++ b/solution.py
@@ -65,9 +65,10 @@
 
 def kernel(
     start_hbm, end_hbm, levels_hbm, gate_hbm, q_hbm, k_hbm, v_hbm, latent_hbm,
-    att_hbm, lat_out_hbm, gate_ref,
+    out_hbm,
+    att_buf, lat_buf, out_buf, gate_row,
     q_buf, k_buf, v_buf, o_buf, gate_buf, start_ref, end_ref, levels_ref,
-    in_send, in_recv, near_send, near_recv, o_send, o_recv, lat_send, lat_recv, table_sem,
+    in_send, in_recv, near_send, near_recv, o_send, o_recv, lat_send, lat_recv, table_sem, out_sem,
 ):
     x, y, z, core = position()
     z_lo, z_hi = lax.rem(z, 4), z // 4
@@ -146,7 +147,7 @@
         width = latent_hbm.shape[1] // LAT_PARTS
         columns = pl.ds(pl.multiple_of(part * width, HEAD_DIM), width)
         return pltpu.make_async_remote_copy(
-            src_ref=latent_hbm.at[:, columns], dst_ref=lat_out_hbm.at[:, columns],
+            src_ref=latent_hbm.at[:, columns], dst_ref=lat_buf.at[:, columns],
             send_sem=lat_send.at[part], recv_sem=lat_recv.at[part],
             device_id=home(home_after, here), device_id_type=MESH,
         )
@@ -175,7 +176,7 @@
     def o_copy(h, t):
         return pltpu.make_async_remote_copy(
             src_ref=o_buf.at[h, pl.ds(pl.multiple_of(t * SLICE, SLICE), SLICE)],
-            dst_ref=att_hbm.at[:, pl.ds(pl.multiple_of(z * GROUP + h * HEAD_DIM, HEAD_DIM), HEAD_DIM)],
+            dst_ref=att_buf.at[:, pl.ds(pl.multiple_of(z * GROUP + h * HEAD_DIM, HEAD_DIM), HEAD_DIM)],
             send_sem=o_send.at[h, t], recv_sem=o_recv.at[h],
             device_id=home(after, t), device_id_type=MESH,
         )
@@ -192,7 +193,7 @@
     for copy in tables:
         copy.wait()
     level = levels_ref[wrap(lax.axis_index("frame") - 1, 64)]
-    gate_ref[...] = jnp.broadcast_to(gate_buf[pl.ds(level, 1), :], gate_ref.shape)
+    gate_row[...] = jnp.broadcast_to(gate_buf[pl.ds(level, 1), :], gate_row.shape)
 
     column = lax.broadcasted_iota(jnp.int32, (1, BLOCK), 1)
     first = start_ref[block] * FRAME_TOK
@@ -247,18 +248,28 @@
     lax.fori_loop(0, LOCAL_HEADS * CHUNKS, step, 0)
 
     for h in range(LOCAL_HEADS):
-        pltpu.make_async_copy(o_buf.at[h], o_buf.at[h], o_recv.at[h]).wait()
-    for part in range(LAT_PARTS):
-        lat_copy(part).wait()
-    for h in range(LOCAL_HEADS):
-        for t in range(8):
-            o_copy(h, t).wait_send()
         for which in range(3):
             for i in range(PEERS):
                 served(i, lambda: None, lambda: in_copy(which, h, i).wait_send())
             if which < 2:
                 for side in range(2):
                     near_copy(which, h, side).wait_send()
+    for part in range(LAT_PARTS):
+        lat_copy(part).wait()
+    moved = lax.axis_index("frame") > 0
+    for h in range(LOCAL_HEADS):
+        for t in range(PEERS):
+            o_copy(h, t).wait_send()
+        pltpu.make_async_copy(o_buf.at[h], o_buf.at[h], o_recv.at[h]).wait()
+        for group in range(PEERS):
+            columns = pl.ds(group * GROUP + h * HEAD_DIM, HEAD_DIM)
+            updated = lat_buf[:, columns].astype(jnp.float32) + gate_row[0:1, columns] * att_buf[
+                :, columns
+            ].astype(jnp.float32)
+            out_buf[:, columns] = jnp.where(moved, updated, 0.0).astype(jnp.bfloat16)
+    done = pltpu.make_async_copy(out_buf, out_hbm, out_sem)
+    done.start()
+    done.wait()
 
 
 def run_kernel(
@@ -269,10 +280,14 @@
     rows = jax.ShapeDtypeStruct(latent.shape, jnp.bfloat16)
     return pl.pallas_call(
         kernel,
-        out_shape=(rows, rows, jax.ShapeDtypeStruct((8, step_gate.shape[1]), jnp.float32)),
+        out_shape=rows,
         in_specs=[any_spec] * 8,
-        out_specs=(any_spec, any_spec, pl.BlockSpec(memory_space=pltpu.VMEM)),
+        out_specs=any_spec,
         scratch_shapes=[
+            pltpu.VMEM(rows.shape, jnp.bfloat16),
+            pltpu.VMEM(rows.shape, jnp.bfloat16),
+            pltpu.VMEM(rows.shape, jnp.bfloat16),
+            pltpu.VMEM((8, step_gate.shape[1]), jnp.float32),
             pltpu.VMEM((LOCAL_HEADS, BLOCK, HEAD_DIM), jnp.bfloat16),
             pltpu.VMEM((LOCAL_HEADS, 3 * BLOCK, HEAD_DIM), jnp.bfloat16),
             pltpu.VMEM((LOCAL_HEADS, 3 * BLOCK, HEAD_DIM), jnp.bfloat16),
@@ -284,7 +299,7 @@
             dma((3, LOCAL_HEADS, 8)), dma((3, LOCAL_HEADS)),
             dma((2, LOCAL_HEADS, 2)), dma((2, LOCAL_HEADS, 2)),
             dma((LOCAL_HEADS, 8)), dma((LOCAL_HEADS,)),
-            dma((LAT_PARTS,)), dma((LAT_PARTS,)), dma((4,)),
+            dma((LAT_PARTS,)), dma((LAT_PARTS,)), dma((4,)), dma,
         ],
         compiler_params=pltpu.CompilerParams(
             collective_id=cid, has_side_effects=True, vmem_limit_bytes=61000 << 10
@@ -297,13 +312,7 @@
 
 
 def on_device(queries, keys, values, latent, step_gate, levels, context_start, context_end):
-    attended, moved, gate = run_kernel(
-        context_start, context_end, queries, keys, values, latent, step_gate, levels
-    )
-    tiles = (latent.shape[0] // 8, 8, latent.shape[1])
-    updated = moved.reshape(tiles).astype(jnp.float32) + gate * attended.reshape(tiles).astype(jnp.float32)
-    queued = jnp.where(lax.axis_index("frame") > 0, updated, 0.0).astype(jnp.bfloat16)
-    return queued.reshape(latent.shape)
+    return run_kernel(context_start, context_end, queries, keys, values, latent, step_gate, levels)
 
 
 def solution(mesh):

time: 104 us -> 104 us (level)
  other arithmetic: 2.54 us -> 0 us
  local copies, waits for them, and re-layouts: 0 us -> 2.06 us
    convert_element_type x1 -> x0, other arithmetic: 2.54 us -> none  [on_device(): jnp.where(lax.axis_index('frame') > 0, updated, 0.0).astype(jnp.bfloat16)]
    unnamed x0 -> x1, local copies, waits for them, and re-layouts: none -> 2.06 us
where the time goes in v5:
time: 104 us; the launch traced here: 103 us
  Pallas kernels  101 us (97%)
  local copies, waits for them, and re-layouts  2.06 us (2%)
    pallas_call x1, Pallas kernels, run_kernel(): pl.pallas_call(kernel, out_shape=rows, in_specs=[any_spec] * 8, out_specs...  101 us

profile of v5, /device:TPU:1, one launch (start us, length us, event | category | flops | bytes accessed | tf_op | source)
XLA Modules:
  0.0 103.3 jit_solution(8684928721990050344)
XLA Ops:
  0.0 101.2 %attend.1 = bf16[128,3072]{1,0:T(8,128)(2,1)} custom-call(s32[64]{0:T(128)} %start_hbm.1, s32[64]{0:T(128)} %end_hbm.1, s32[64]{0:T(128)} %levels_hbm.1, f32[50,3072]{1,0:T(8,128)} %gate_hbm.1, bf16[128,3072]{1,0:T(8,128)(2,1)} %q_hbm.1, bf16[128,3072]{1,0:T(8,128)(2,1)} %k_hbm.1, bf16[128,3072]{1,0:T(8,128)(2,1)} %v_hbm.1, bf16[128,3072]{1,0:T(8,128)(2,1)} %latent_hbm.1), custom_call_target="tpu_custom_call" | custom-call | flops 4831838208 | bytes 8388608 | tf_op jit(solution)/shard_map/attend/pallas_call | solution.py:281
  101.2 2.1 %copy.10 = bf16[128,3072]{1,0:T(8,128)(2,1)} copy(bf16[128,3072]{1,0:T(8,128)(2,1)} %attend.1) | data formatting | bytes 1572864

commit v6 on v5

--- a/solution.py
+++ b/solution.py
@@ -56,7 +56,7 @@
 
 
 def offset(group):
-    return 2 * lax.rem(group, 2)
+    return 2 * lax.rem(group, 2) + group // 4
 
 
 def worker(pair, y, core, group):
@@ -184,12 +184,11 @@
     for h in range(LOCAL_HEADS):
         for which in (KEYS, VALUES, QUERIES):
             send_in(which, h)
-            if which == VALUES:
-                lat_copy(h).start()
     for copy in tables:
         copy.start()
     pass_on(KEYS, 0)
     pass_on(VALUES, 0)
+    lat_copy(0).start()
     for copy in tables:
         copy.wait()
     level = levels_ref[wrap(lax.axis_index("frame") - 1, 64)]
@@ -218,6 +217,7 @@
         @pl.when((i == 3) & (h < LOCAL_HEADS - 1))
         def _():
             pass_on(VALUES, h + 1)
+            lat_copy(h + 1).start()
 
         chunk = lax.rem(i + x + z, CHUNKS)
         rows = pl.ds(pl.multiple_of(chunk * Q_ROWS, Q_ROWS), Q_ROWS)

time: 104 us -> 102 us (0.981)
  Pallas kernels: 101 us -> 99.5 us
    pallas_call x1, Pallas kernels: 101 us -> 99.5 us  [run_kernel(): pl.pallas_call(kernel, out_shape=rows, in_specs=[any_spec] * 8, out_specs...]
where the time goes in v6:
time: 102 us
  Pallas kernels  99.5 us (98%)
  local copies, waits for them, and re-layouts  2.06 us (2%)
    pallas_call x1, Pallas kernels, run_kernel(): pl.pallas_call(kernel, out_shape=rows, in_specs=[any_spec] * 8, out_specs...  99.5 us
    unnamed x1, local copies, waits for them, and re-layouts  2.06 us

profile of v6, /device:TPU:1, one launch (start us, length us, event | category | flops | bytes accessed | tf_op | source)
XLA Modules:
  0.0 101.6 jit_solution(3123884332457906790)
XLA Ops:
  0.0 99.5 %attend.1 = bf16[128,3072]{1,0:T(8,128)(2,1)} custom-call(s32[64]{0:T(128)} %start_hbm.1, s32[64]{0:T(128)} %end_hbm.1, s32[64]{0:T(128)} %levels_hbm.1, f32[50,3072]{1,0:T(8,128)} %gate_hbm.1, bf16[128,3072]{1,0:T(8,128)(2,1)} %q_hbm.1, bf16[128,3072]{1,0:T(8,128)(2,1)} %k_hbm.1, bf16[128,3072]{1,0:T(8,128)(2,1)} %v_hbm.1, bf16[128,3072]{1,0:T(8,128)(2,1)} %latent_hbm.1), custom_call_target="tpu_custom_call" | custom-call | flops 4831838208 | bytes 8388608 | tf_op jit(solution)/shard_map/attend/pallas_call | solution.py:281
  99.5 2.1 %copy.10 = bf16[128,3072]{1,0:T(8,128)(2,1)} copy(bf16[128,3072]{1,0:T(8,128)(2,1)} %attend.1) | data formatting | bytes 1572864
